TPU v7x, 32 devices: a whole 2x2x4 slice. The times are simulated.
32 devices in a mesh: stripe: 8 (over z, core), tile: 4 (over y, x).
Axes of the slice: x: 2, y: 2, z: 4, core: 2. Of those that a mesh axis runs over, the one named last changes fastest.
Arguments:
- positions: int32 [8, 12], P('stripe', 'tile'), may hold values from -64 to -64, as said below
- row_offsets: int32 [8, 12], P('stripe', 'tile'), may hold values from -64 to 64, as said below
- amplitudes: float32 [8, 12, 256, 256], P('stripe', 'tile'), may hold values from 0 to 2
- object_field: float32 [2, 2048, 512], P(None, 'stripe', 'tile'), may hold values from -6 to 6
- probe_field: float32 [2, 256, 256], replicated, may hold values from -6 to 6
Outputs:
- object_out: float32 [2, 2048, 512], P(None, 'stripe', 'tile')
- probe_out: float32 [2, 256, 256], replicated
Inputs may be any that keep to these rules, and one draw needn't show every extreme that they name: `positions`: in every block of 3 patterns of one stripe and one tile, the first offset is -64 and the second is 128 - 192. `row_offsets`: in every block of 3 patterns of one stripe and one tile, the first row offset is -64 and the second is 64.
All inputs are finite; a program needn't handle non-finite values.
Results may differ from a plain program's by a relative error of at most 0.0006.
The roundings to bfloat16 on the way count: a program that leaves them out, or rounds other values in their place, can miss the bound.
Values sent between devices are 32-bit elements; how exact they have to be, the bound alone decides.
A program may use at most 64 MiB of HBM per device.

v0:
```python
import math

import jax
import jax.numpy as jnp
from jax import lax
from jax.sharding import PartitionSpec as P

PW = 256
HALO = 64
TILE_W = 128
PAT_DEV = 3
INNER = 2
OUTER = 2


def padded(x, sides, width):
    for axis, dim in sides:
        count, length = (lax.axis_size(axis), x.shape[dim])
        up = [(i, (i + 1) % count) for i in range(count - 1)]
        down = [(j, i) for i, j in up]
        last = lax.slice_in_dim(x, length - width, length, axis=dim)
        first = lax.slice_in_dim(x, 0, width, axis=dim)
        before = lax.ppermute(last, axis, up)
        after = lax.ppermute(first, axis, down)
        x = jnp.concatenate([before, x, after], axis=dim)
    return x


def from_behind(value, axis, steps):
    count = lax.axis_size(axis)
    first, last = (max(0, -steps), min(count, count - steps))
    return lax.ppermute(value, axis, [(source, source + steps) for source in range(first, last)])


def dft_tables():
    indices = jnp.arange(PW, dtype=jnp.int32)
    phase = indices[:, None] * indices[None, :] % PW
    angles = phase.astype(jnp.float32) * (2.0 * math.pi / PW)
    factor = 1.0 / math.sqrt(PW)
    return (
        (jnp.cos(angles) * factor).astype(jnp.bfloat16),
        (jnp.sin(angles) * factor).astype(jnp.bfloat16),
    )


def apply_left(matrix, batch):
    return jnp.einsum("kn,pnm->pkm", matrix, batch, preferred_element_type=jnp.float32)


def apply_right(batch, matrix):
    return jnp.einsum("pkn,nm->pkm", batch, matrix, preferred_element_type=jnp.float32)


def pattern_pass(windows, probe_field, measured, cosine, sine):
    win_re = windows[:, 0]
    win_im = windows[:, 1]
    probe_re = probe_field[0]
    probe_im = probe_field[1]
    exit_re = (probe_re * win_re - probe_im * win_im).astype(jnp.bfloat16)
    exit_im = (probe_re * win_im + probe_im * win_re).astype(jnp.bfloat16)
    half_re = (apply_left(cosine, exit_re) + apply_left(sine, exit_im)).astype(jnp.bfloat16)
    half_im = (apply_left(cosine, exit_im) - apply_left(sine, exit_re)).astype(jnp.bfloat16)
    spec_re = apply_right(half_re, cosine) + apply_right(half_im, sine)
    spec_im = apply_right(half_im, cosine) - apply_right(half_re, sine)
    magnitude = jnp.sqrt(spec_re * spec_re + spec_im * spec_im)
    scaling = measured / jnp.maximum(magnitude, 0.5)
    miss_re = (spec_re - scaling * spec_re).astype(jnp.bfloat16)
    miss_im = (spec_im - scaling * spec_im).astype(jnp.bfloat16)
    hb_re = (apply_left(cosine, miss_re) - apply_left(sine, miss_im)).astype(jnp.bfloat16)
    hb_im = (apply_left(cosine, miss_im) + apply_left(sine, miss_re)).astype(jnp.bfloat16)
    back_re = apply_right(hb_re, cosine) - apply_right(hb_im, sine)
    back_im = apply_right(hb_im, cosine) + apply_right(hb_re, sine)
    object_grad = jnp.stack(
        [probe_re * back_re + probe_im * back_im, probe_re * back_im - probe_im * back_re], axis=1
    )
    probe_grad = jnp.stack(
        [
            jnp.sum(win_re * back_re + win_im * back_im, axis=0),
            jnp.sum(win_re * back_im - win_im * back_re, axis=0),
        ]
    )
    illumination = jnp.sum(win_re * win_re + win_im * win_im, axis=0)
    return (object_grad, probe_grad, illumination)


def per_device(positions, row_offsets, amplitudes, object_field, probe_field):
    cosine, sine = dft_tables()
    column_starts = positions[0] + HALO
    row_starts = row_offsets[0] + HALO
    measured = amplitudes[0]
    rows_ext = PW + 2 * HALO
    columns_ext = TILE_W + 2 * HALO
    zero_index = jnp.zeros((), jnp.int32)
    current = object_field
    extended = object_field
    for outer_step in range(OUTER):
        grad_sum = jnp.zeros((2, PW, PW), jnp.float32)
        light_sum = jnp.zeros((PW, PW), jnp.float32)
        step_size = 1.0 / (
            2.0
            * PAT_DEV
            * jnp.max(probe_field[0] * probe_field[0] + probe_field[1] * probe_field[1])
            + 1e-06
        )
        for inner_step in range(INNER):
            extended = padded(current, (("stripe", 1), ("tile", 2)), HALO)
            windows = jax.vmap(
                lambda row_start, column_start: lax.dynamic_slice(
                    extended, (zero_index, row_start, column_start), (2, PW, PW)
                )
            )(row_starts, column_starts)
            object_grad, grad_sum, light_sum = pattern_pass(
                windows, probe_field, measured, cosine, sine
            )
            gradient = jnp.zeros((2, rows_ext, columns_ext), jnp.float32)
            for pattern in range(PAT_DEV):
                where = (zero_index, row_starts[pattern], column_starts[pattern])
                before = lax.dynamic_slice(gradient, where, (2, PW, PW))
                gradient = lax.dynamic_update_slice(gradient, before + object_grad[pattern], where)
            from_left = from_behind(gradient[:, :, HALO + TILE_W :], "tile", 1)
            from_right = from_behind(gradient[:, :, :HALO], "tile", -1)
            middle = gradient[:, :, HALO : HALO + TILE_W]
            middle = middle.at[:, :, :HALO].add(from_left)
            middle = middle.at[:, :, TILE_W - HALO :].add(from_right)
            from_above = from_behind(middle[:, HALO + PW :, :], "stripe", 1)
            from_below = from_behind(middle[:, :HALO, :], "stripe", -1)
            own_grad = middle[:, HALO : HALO + PW, :]
            own_grad = own_grad.at[:, :HALO, :].add(from_above)
            own_grad = own_grad.at[:, PW - HALO :, :].add(from_below)
            current = current - step_size * own_grad
        row_count = PW // lax.axis_size("tile")
        share_grad, share_light = (
            lax.psum_scatter(grad_sum, "tile", scatter_dimension=1, tiled=True),
            lax.psum_scatter(light_sum[None], "tile", scatter_dimension=1, tiled=True),
        )
        share_grad, share_light = lax.psum((share_grad, share_light), "stripe")
        own_rows = lax.dynamic_slice_in_dim(
            probe_field, lax.axis_index("tile") * row_count, row_count, 1
        )
        new_rows = own_rows - 0.5 * share_grad / (share_light + 1.0)
        probe_field = lax.all_gather(new_rows, "tile", axis=1, tiled=True)
    return (current, probe_field)


def solution(mesh):
    placed = (
        P("stripe", "tile"),
        P("stripe", "tile"),
        P("stripe", "tile", None, None),
        P(None, "stripe", "tile"),
        P(),
    )
    return jax.shard_map(
        per_device,
        mesh=mesh,
        in_specs=placed,
        out_specs=(P(None, "stripe", "tile"), P()),
        check_vma=False,
    )
```

profile of v0, /device:TPU:0, one launch (start us, length us, event | category | flops | bytes accessed | tf_op | source)
XLA Modules:
  0.0 558.9 jit_solution(618792989094165680)
XLA Ops:
  25.5 6.6 %collective-permute-done.2 = f32[2,384,64]{2,0,1:T(2,128)S(1)} collective-permute-done((f32[2,384,64]{2,0,1:T(2,128)S(1)}, f32[2,384,64]{2,0,1:T(2,128)S(1)}, u32[]{:S(2)}, u32[]{:S(2)}) %collective-permute-start.2) | collective-permute-done | bytes 196640 | tf_op jit(solution)/shard_map/ppermute | solution.py:23
  32.1 10.4 %collective-permute-done.3 = f32[2,384,64]{2,0,1:T(2,128)S(1)} collective-permute-done((f32[2,384,64]{2,0,1:T(2,128)S(1)}, f32[2,384,64]{2,0,1:T(2,128)S(1)}, u32[]{:S(2)}, u32[]{:S(2)}) %collective-permute-start.3) | collective-permute-done | bytes 196640 | tf_op jit(solution)/shard_map/ppermute | solution.py:24
  66.8 12.6 %subtract_bitcast_fusion.3 = (f32[3,1,256,256]{3,2,0,1:T(8,128)S(1)}, f32[3,1,256,256]{3,2,0,1:T(8,128)S(1)}) fusion(f32[3,256,256]{2,1,0:T(8,128)S(1)} %convolution_add_fusion.12, f32[256,256]{1,0:T(8,128)S(1)} %get-tuple-element.251, f32[256,256]{1,0:T(8,128)S(1)} %get-tuple-element.250, f32[3,256,256]{2,1,0:T(8,128)S(1)} %fusion.160, ...), kind=kOutput, calls=%fused_computation.134 | convolution fusion | flops 103088128 | bytes 4063232 | tf_op jit(solution)/shard_map/pkn,nm->pkm/dot_general | solution.py:51
  92.6 8.0 %collective-permute-done.4 = f32[2,384,64]{2,1,0:T(8,128)S(1)} collective-permute-done((f32[2,384,64]{2,1,0:T(8,128)S(1)}, f32[2,384,64]{2,1,0:T(8,128)S(1)}, u32[]{:S(2)}, u32[]{:S(2)}) %collective-permute-start.4) | collective-permute-done | bytes 196640 | tf_op jit(solution)/shard_map/ppermute | solution.py:32
  101.7 7.5 %collective-permute-done.5 = f32[2,384,64]{2,1,0:T(8,128)S(1)} collective-permute-done((f32[2,384,64]{2,1,0:T(8,128)S(1)}, f32[2,384,64]{2,1,0:T(8,128)S(1)}, u32[]{:S(2)}, u32[]{:S(2)}) %collective-permute-start.5) | collective-permute-done | bytes 196640 | tf_op jit(solution)/shard_map/ppermute | solution.py:32
  120.5 4.8 collective-permute-start.8
  131.5 6.3 %collective-permute-done.10 = f32[2,384,64]{2,1,0:T(8,128)S(1)} collective-permute-done((f32[2,384,64]{2,1,0:T(8,128)S(1)}, f32[2,384,64]{2,1,0:T(8,128)S(1)}, u32[]{:S(2)}, u32[]{:S(2)}) %collective-permute-start.10) | collective-permute-done | bytes 196640 | tf_op jit(solution)/shard_map/ppermute | solution.py:23
  137.8 8.7 %collective-permute-done.11 = f32[2,384,64]{2,1,0:T(8,128)S(1)} collective-permute-done((f32[2,384,64]{2,1,0:T(8,128)S(1)}, f32[2,384,64]{2,1,0:T(8,128)S(1)}, u32[]{:S(2)}, u32[]{:S(2)}) %collective-permute-start.11) | collective-permute-done | bytes 196640 | tf_op jit(solution)/shard_map/ppermute | solution.py:24
  184.8 7.6 %collective-permute-done.12 = f32[2,384,64]{2,1,0:T(8,128)S(1)} collective-permute-done((f32[2,384,64]{2,1,0:T(8,128)S(1)}, f32[2,384,64]{2,1,0:T(8,128)S(1)}, u32[]{:S(2)}, u32[]{:S(2)}) %collective-permute-start.12) | collective-permute-done | bytes 196640 | tf_op jit(solution)/shard_map/ppermute | solution.py:32
  193.5 8.4 %collective-permute-done.13 = f32[2,384,64]{2,1,0:T(8,128)S(1)} collective-permute-done((f32[2,384,64]{2,1,0:T(8,128)S(1)}, f32[2,384,64]{2,1,0:T(8,128)S(1)}, u32[]{:S(2)}, u32[]{:S(2)}) %collective-permute-start.13) | collective-permute-done | bytes 196640 | tf_op jit(solution)/shard_map/ppermute | solution.py:32
  213.7 4.8 collective-permute-start.16
  224.7 6.1 %collective-permute-done.18 = f32[2,384,64]{2,1,0:T(8,128)S(1)} collective-permute-done((f32[2,384,64]{2,1,0:T(8,128)S(1)}, f32[2,384,64]{2,1,0:T(8,128)S(1)}, u32[]{:S(2)}, u32[]{:S(2)}) %collective-permute-start.18) | collective-permute-done | bytes 196640 | tf_op jit(solution)/shard_map/ppermute | solution.py:23
  230.8 10.9 %collective-permute-done.19 = f32[2,384,64]{2,1,0:T(8,128)S(1)} collective-permute-done((f32[2,384,64]{2,1,0:T(8,128)S(1)}, f32[2,384,64]{2,1,0:T(8,128)S(1)}, u32[]{:S(2)}, u32[]{:S(2)}) %collective-permute-start.19) | collective-permute-done | bytes 196640 | tf_op jit(solution)/shard_map/ppermute | solution.py:24
  247.5 52.1 %all-reduce.7.cloned.1.call-done = (f32[2,64,256]{2,1,0:T(8,128)}, f32[1,64,256]{2,1,0:T(8,128)}) async-done(((f32[2,64,256]{2,1,0:T(8,128)}, f32[1,64,256]{2,1,0:T(8,128)}), (f32[2,64,256]{2,1,0:T(8,128)}, f32[1,64,256]{2,1,0:T(8,128)})) %all-reduce.7.cloned.1.call-update) | async-done | bytes 196624 | tf_op jit(solution)/shard_map/psum | solution.py:136
  301.5 10.9 %all_gather.6 = f32[2,256,256]{2,1,0:T(8,128)S(1)} all-gather(f32[2,64,256]{2,1,0:T(8,128)S(1)} %divide_subtract_fusion.1), channel_id=1, replica_groups=mesh['stripe'=8,'tile'=4] {'tile'}, dimensions={1}, use_global_device_ids=true | all-gather | bytes 655360 | tf_op jit(solution)/shard_map/all_gather | solution.py:141
  357.3 8.8 %collective-permute-done.21 = f32[2,384,64]{2,1,0:T(8,128)S(1)} collective-permute-done((f32[2,384,64]{2,1,0:T(8,128)S(1)}, f32[2,384,64]{2,1,0:T(8,128)S(1)}, u32[]{:S(2)}, u32[]{:S(2)}) %collective-permute-start.21) | collective-permute-done | bytes 196640 | tf_op jit(solution)/shard_map/ppermute | solution.py:32
  387.1 6.4 %collective-permute-done.26 = f32[2,384,64]{2,1,0:T(8,128)S(1)} collective-permute-done((f32[2,384,64]{2,1,0:T(8,128)S(1)}, f32[2,384,64]{2,1,0:T(8,128)S(1)}, u32[]{:S(2)}, u32[]{:S(2)}) %collective-permute-start.26) | collective-permute-done | bytes 196640 | tf_op jit(solution)/shard_map/ppermute | solution.py:23
  393.5 8.6 %collective-permute-done.27 = f32[2,384,64]{2,1,0:T(8,128)S(1)} collective-permute-done((f32[2,384,64]{2,1,0:T(8,128)S(1)}, f32[2,384,64]{2,1,0:T(8,128)S(1)}, u32[]{:S(2)}, u32[]{:S(2)}) %collective-permute-start.27) | collective-permute-done | bytes 196640 | tf_op jit(solution)/shard_map/ppermute | solution.py:24
  442.1 6.6 %collective-permute-done.28 = f32[2,384,64]{2,1,0:T(8,128)S(1)} collective-permute-done((f32[2,384,64]{2,1,0:T(8,128)}, f32[2,384,64]{2,1,0:T(8,128)S(1)}, u32[]{:S(2)}, u32[]{:S(2)}) %collective-permute-start.28) | collective-permute-done | bytes 196640 | tf_op jit(solution)/shard_map/ppermute | solution.py:32
  449.8 8.8 %collective-permute-done.29 = f32[2,384,64]{2,1,0:T(8,128)S(1)} collective-permute-done((f32[2,384,64]{2,1,0:T(8,128)S(1)}, f32[2,384,64]{2,1,0:T(8,128)S(1)}, u32[]{:S(2)}, u32[]{:S(2)}) %collective-permute-start.29) | collective-permute-done | bytes 196640 | tf_op jit(solution)/shard_map/ppermute | solution.py:32
  464.1 4.9 collective-permute-done.31
  469.1 12.1 %reduce-scatter.9.cloned.1.call-done = f32[2,64,256]{2,1,0:T(8,128)} async-done(((f32[2,256,256]{2,1,0:T(8,128)}), f32[2,64,256]{2,1,0:T(8,128)}) %reduce-scatter.9.cloned.1.call-update) | async-done | bytes 131088 | tf_op jit(solution)/shard_map/reduce_scatter | solution.py:133
  482.0 56.4 %all-reduce.5.cloned.1.call-done = (f32[2,64,256]{2,1,0:T(8,128)}, f32[1,64,256]{2,1,0:T(8,128)}) async-done(((f32[2,64,256]{2,1,0:T(8,128)}, f32[1,64,256]{2,1,0:T(8,128)}), (f32[2,64,256]{2,1,0:T(8,128)}, f32[1,64,256]{2,1,0:T(8,128)})) %all-reduce.5.cloned.1.call-update) | async-done | bytes 196624 | tf_op jit(solution)/shard_map/psum | solution.py:136
  540.1 10.7 %all_gather.7 = f32[2,256,256]{2,1,0:T(8,128)S(1)} all-gather(f32[2,64,256]{2,1,0:T(8,128)S(1)} %divide_subtract_fusion), channel_id=1, replica_groups=mesh['stripe'=8,'tile'=4] {'tile'}, dimensions={1}, use_global_device_ids=true | all-gather | bytes 655360 | tf_op jit(solution)/shard_map/all_gather | solution.py:141
  (279 shorter events, 246.7 us)
Async XLA Ops:
  7.2 238.1 %reduce-scatter.7.cloned.1.call-start = ((), (), s32[]{:S(2)}) async-start(), calls=%async_computation.5 | async-start | bytes 327680 | tf_op jit(solution)/shard_map/reduce_scatter | solution.py:134
  8.2 11.0 %collective-permute-start = (f32[2,64,128]{2,0,1:T(2,128)S(1)}, f32[2,64,128]{2,0,1:T(2,128)S(1)}, u32[]{:S(2)}, u32[]{:S(2)}) collective-permute-start(f32[2,64,128]{2,0,1:T(2,128)S(1)} %copy.230), channel_id=1, source_target_pairs={{0,4},{4,8},{8,12},{12,16},{16,20},{20,24},{24,28},{1,5},{5,9},{9,... | collective-permute-start | bytes 196616 | tf_op jit(solution)/shard_map/ppermute | solution.py:23
  10.6 8.8 %collective-permute-start.1 = (f32[2,64,128]{2,0,1:T(2,128)S(1)}, f32[2,64,128]{2,0,1:T(2,128)S(1)}, u32[]{:S(2)}, u32[]{:S(2)}) collective-permute-start(f32[2,64,128]{2,0,1:T(2,128)S(1)} %copy.231), channel_id=1, source_target_pairs={{4,0},{8,4},{12,8},{16,12},{20,16},{24,20},{28,24},{5,1},{9,5},{13... | collective-permute-start | bytes 196616 | tf_op jit(solution)/shard_map/ppermute | solution.py:24
  19.9 12.1 %collective-permute-start.2 = (f32[2,384,64]{2,0,1:T(2,128)S(1)}, f32[2,384,64]{2,0,1:T(2,128)S(1)}, u32[]{:S(2)}, u32[]{:S(2)}) collective-permute-start(f32[2,384,64]{2,0,1:T(2,128)S(1)} %get-tuple-element.266), channel_id=1, source_target_pairs={{0,1},{1,2},{2,3},{4,5},{5,6},{6,7},{8,9},{9,10},{10,11},{12,13},{... | collective-permute-start | bytes 589832 | tf_op jit(solution)/shard_map/ppermute | solution.py:23
  24.2 18.3 %collective-permute-start.3 = (f32[2,384,64]{2,0,1:T(2,128)S(1)}, f32[2,384,64]{2,0,1:T(2,128)S(1)}, u32[]{:S(2)}, u32[]{:S(2)}) collective-permute-start(f32[2,384,64]{2,0,1:T(2,128)S(1)} %get-tuple-element.267), channel_id=1, source_target_pairs={{1,0},{2,1},{3,2},{5,4},{6,5},{7,6},{9,8},{10,9},{11,10},{13,12},{... | collective-permute-start | bytes 589832 | tf_op jit(solution)/shard_map/ppermute | solution.py:24
  87.6 13.0 %collective-permute-start.4 = (f32[2,384,64]{2,1,0:T(8,128)S(1)}, f32[2,384,64]{2,1,0:T(8,128)S(1)}, u32[]{:S(2)}, u32[]{:S(2)}) collective-permute-start(f32[2,384,64]{2,1,0:T(8,128)S(1)} %get-tuple-element.247), channel_id=1, source_target_pairs={{0,1},{1,2},{2,3},{4,5},{5,6},{6,7},{8,9},{9,10},{10,11},{12,13},{... | collective-permute-start | bytes 589832 | tf_op jit(solution)/shard_map/ppermute | solution.py:32
  91.3 17.9 %collective-permute-start.5 = (f32[2,384,64]{2,1,0:T(8,128)S(1)}, f32[2,384,64]{2,1,0:T(8,128)S(1)}, u32[]{:S(2)}, u32[]{:S(2)}) collective-permute-start(f32[2,384,64]{2,1,0:T(8,128)S(1)} %get-tuple-element.246), channel_id=1, source_target_pairs={{1,0},{2,1},{3,2},{5,4},{6,5},{7,6},{9,8},{10,9},{11,10},{13,12},{... | collective-permute-start | bytes 589832 | tf_op jit(solution)/shard_map/ppermute | solution.py:32
  128.7 9.1 %collective-permute-start.10 = (f32[2,384,64]{2,1,0:T(8,128)S(1)}, f32[2,384,64]{2,1,0:T(8,128)S(1)}, u32[]{:S(2)}, u32[]{:S(2)}) collective-permute-start(f32[2,384,64]{2,1,0:T(8,128)S(1)} %get-tuple-element.262), channel_id=1, source_target_pairs={{0,1},{1,2},{2,3},{4,5},{5,6},{6,7},{8,9},{9,10},{10,11},{12,13},{... | collective-permute-start | bytes 589832 | tf_op jit(solution)/shard_map/ppermute | solution.py:23
  130.2 16.3 %collective-permute-start.11 = (f32[2,384,64]{2,1,0:T(8,128)S(1)}, f32[2,384,64]{2,1,0:T(8,128)S(1)}, u32[]{:S(2)}, u32[]{:S(2)}) collective-permute-start(f32[2,384,64]{2,1,0:T(8,128)S(1)} %get-tuple-element.263), channel_id=1, source_target_pairs={{1,0},{2,1},{3,2},{5,4},{6,5},{7,6},{9,8},{10,9},{11,10},{13,12},{... | collective-permute-start | bytes 589832 | tf_op jit(solution)/shard_map/ppermute | solution.py:24
  181.7 10.7 %collective-permute-start.12 = (f32[2,384,64]{2,1,0:T(8,128)S(1)}, f32[2,384,64]{2,1,0:T(8,128)S(1)}, u32[]{:S(2)}, u32[]{:S(2)}) collective-permute-start(f32[2,384,64]{2,1,0:T(8,128)S(1)} %get-tuple-element.245), channel_id=1, source_target_pairs={{0,1},{1,2},{2,3},{4,5},{5,6},{6,7},{8,9},{9,10},{10,11},{12,13},{... | collective-permute-start | bytes 589832 | tf_op jit(solution)/shard_map/ppermute | solution.py:32
  183.5 61.9 %reduce-scatter.5.cloned.1.call-start = ((), (), s32[]{:S(2)}) async-start(), calls=%async_computation.4 | async-start | bytes 655360 | tf_op jit(solution)/shard_map/reduce_scatter | solution.py:133
  183.5 18.5 %collective-permute-start.13 = (f32[2,384,64]{2,1,0:T(8,128)S(1)}, f32[2,384,64]{2,1,0:T(8,128)S(1)}, u32[]{:S(2)}, u32[]{:S(2)}) collective-permute-start(f32[2,384,64]{2,1,0:T(8,128)S(1)} %get-tuple-element.244), channel_id=1, source_target_pairs={{1,0},{2,1},{3,2},{5,4},{6,5},{7,6},{9,8},{10,9},{11,10},{13,12},{... | collective-permute-start | bytes 589832 | tf_op jit(solution)/shard_map/ppermute | solution.py:32
  207.4 92.2 %all-reduce.7.cloned.1.call-start = ((), (), s32[]{:S(2)}) async-start(), calls=%async_computation.9 | async-start | bytes 393216 | tf_op jit(solution)/shard_map/psum | solution.py:136
  221.9 8.9 %collective-permute-start.18 = (f32[2,384,64]{2,1,0:T(8,128)S(1)}, f32[2,384,64]{2,1,0:T(8,128)S(1)}, u32[]{:S(2)}, u32[]{:S(2)}) collective-permute-start(f32[2,384,64]{2,1,0:T(8,128)S(1)} %get-tuple-element.258), channel_id=1, source_target_pairs={{0,1},{1,2},{2,3},{4,5},{5,6},{6,7},{8,9},{9,10},{10,11},{12,13},{... | collective-permute-start | bytes 589832 | tf_op jit(solution)/shard_map/ppermute | solution.py:23
  223.4 18.3 %collective-permute-start.19 = (f32[2,384,64]{2,1,0:T(8,128)S(1)}, f32[2,384,64]{2,1,0:T(8,128)S(1)}, u32[]{:S(2)}, u32[]{:S(2)}) collective-permute-start(f32[2,384,64]{2,1,0:T(8,128)S(1)} %get-tuple-element.259), channel_id=1, source_target_pairs={{1,0},{2,1},{3,2},{5,4},{6,5},{7,6},{9,8},{10,9},{11,10},{13,12},{... | collective-permute-start | bytes 589832 | tf_op jit(solution)/shard_map/ppermute | solution.py:24
  245.4 223.7 %reduce-scatter.11.cloned.1.call-start = ((), (), s32[]{:S(2)}) async-start(), calls=%async_computation.7 | async-start | bytes 327680 | tf_op jit(solution)/shard_map/reduce_scatter | solution.py:134
  347.7 8.5 %collective-permute-start.20 = (f32[2,384,64]{2,1,0:T(8,128)S(1)}, f32[2,384,64]{2,1,0:T(8,128)S(1)}, u32[]{:S(2)}, u32[]{:S(2)}) collective-permute-start(f32[2,384,64]{2,1,0:T(8,128)S(1)} %get-tuple-element.243), channel_id=1, source_target_pairs={{0,1},{1,2},{2,3},{4,5},{5,6},{6,7},{8,9},{9,10},{10,11},{12,13},{... | collective-permute-start | bytes 589832 | tf_op jit(solution)/shard_map/ppermute | solution.py:32
  351.1 15.0 %collective-permute-start.21 = (f32[2,384,64]{2,1,0:T(8,128)S(1)}, f32[2,384,64]{2,1,0:T(8,128)S(1)}, u32[]{:S(2)}, u32[]{:S(2)}) collective-permute-start(f32[2,384,64]{2,1,0:T(8,128)S(1)} %get-tuple-element.242), channel_id=1, source_target_pairs={{1,0},{2,1},{3,2},{5,4},{6,5},{7,6},{9,8},{10,9},{11,10},{13,12},{... | collective-permute-start | bytes 589832 | tf_op jit(solution)/shard_map/ppermute | solution.py:32
  382.7 10.9 %collective-permute-start.26 = (f32[2,384,64]{2,1,0:T(8,128)S(1)}, f32[2,384,64]{2,1,0:T(8,128)S(1)}, u32[]{:S(2)}, u32[]{:S(2)}) collective-permute-start(f32[2,384,64]{2,1,0:T(8,128)S(1)} %get-tuple-element.254), channel_id=1, source_target_pairs={{0,1},{1,2},{2,3},{4,5},{5,6},{6,7},{8,9},{9,10},{10,11},{12,13},{... | collective-permute-start | bytes 589832 | tf_op jit(solution)/shard_map/ppermute | solution.py:23
  385.6 16.5 %collective-permute-start.27 = (f32[2,384,64]{2,1,0:T(8,128)S(1)}, f32[2,384,64]{2,1,0:T(8,128)S(1)}, u32[]{:S(2)}, u32[]{:S(2)}) collective-permute-start(f32[2,384,64]{2,1,0:T(8,128)S(1)} %get-tuple-element.255), channel_id=1, source_target_pairs={{1,0},{2,1},{3,2},{5,4},{6,5},{7,6},{9,8},{10,9},{11,10},{13,12},{... | collective-permute-start | bytes 589832 | tf_op jit(solution)/shard_map/ppermute | solution.py:24
  429.2 52.1 %reduce-scatter.9.cloned.1.call-start = ((), (), s32[]{:S(2)}) async-start(), calls=%async_computation.6 | async-start | bytes 655360 | tf_op jit(solution)/shard_map/reduce_scatter | solution.py:133
  438.2 10.6 %collective-permute-start.28 = (f32[2,384,64]{2,1,0:T(8,128)}, f32[2,384,64]{2,1,0:T(8,128)S(1)}, u32[]{:S(2)}, u32[]{:S(2)}) collective-permute-start(f32[2,384,64]{2,1,0:T(8,128)} %get-tuple-element.241), channel_id=1, source_target_pairs={{0,1},{1,2},{2,3},{4,5},{5,6},{6,7},{8,9},{9,10},{10,11},{12,13},{... | collective-permute-start | bytes 589832 | tf_op jit(solution)/shard_map/ppermute | solution.py:32
  439.9 18.8 %collective-permute-start.29 = (f32[2,384,64]{2,1,0:T(8,128)S(1)}, f32[2,384,64]{2,1,0:T(8,128)S(1)}, u32[]{:S(2)}, u32[]{:S(2)}) collective-permute-start(f32[2,384,64]{2,1,0:T(8,128)S(1)} %get-tuple-element.240), channel_id=1, source_target_pairs={{1,0},{2,1},{3,2},{5,4},{6,5},{7,6},{9,8},{10,9},{11,10},{13,12},{... | collective-permute-start | bytes 589832 | tf_op jit(solution)/shard_map/ppermute | solution.py:32
  442.1 96.3 %all-reduce.5.cloned.1.call-start = ((), (), s32[]{:S(2)}) async-start(), calls=%async_computation.8 | async-start | bytes 393216 | tf_op jit(solution)/shard_map/psum | solution.py:136
  (31 other events, 338.3 us)
Sparse Core Ops, SparseCore 0:
  183.6 24.0 reduce-scatter.6
  211.3 27.6 reduce-scatter.4
  245.5 54.0 all-reduce.6
  429.3 24.0 reduce-scatter.10
  456.6 24.5 reduce-scatter.8
  483.6 54.7 all-reduce.4
where the time goes:
time: 570 us; the launch traced here: 559 us
  waiting for transfers between devices  267 us (47%)
  matrix products  95.6 us (17%)
  local copies, waits for them, and re-layouts  70 us (12%)
  starting transfers between devices  66.3 us (12%)
  between operations  23.2 us (4%)
  blocking collectives  21.6 us (4%)
  other arithmetic  15.4 us (3%)
    psum x2, waiting for transfers between devices, per_device(): share_grad, share_light = lax.psum((share_grad, share_light), 'stripe')  108 us
    ppermute x16, waiting for transfers between devices, from_behind(): lax.ppermute(value, axis, [(source, source + steps) for source in range(f...  76.5 us
    dot_general x32, matrix products, apply_right(): jnp.einsum('pkn,nm->pkm', batch, matrix, preferred_element_type=jnp.float32)  56.3 us
    ppermute x8, waiting for transfers between devices, padded(): after = lax.ppermute(first, axis, down)  44.1 us
    dot_general x32, matrix products, apply_left(): jnp.einsum('kn,pnm->pkm', matrix, batch, preferred_element_type=jnp.float32)  39.3 us
    dynamic_update_slice x12, local copies, waits for them, and re-layouts, per_device(): lax.dynamic_update_slice(gradient, before + object_grad[pattern], where)  34.8 us
    ppermute x16, starting transfers between devices, from_behind(): lax.ppermute(value, axis, [(source, source + steps) for source in range(f...  28.6 us
    ppermute x8, starting transfers between devices, padded(): before = lax.ppermute(last, axis, up)  27 us
  transfers between devices with their start and end apart: 38, of which 26 were waited for; matrix products, arithmetic and copies ran while one was open for 5% of the time, Pallas kernels for 0%

commit v1 on v0

v1 whole, which is shorter than its diff:
```python
import functools
import math

import jax
import jax.numpy as jnp
import ml_dtypes
import numpy as np
from jax import lax
from jax.experimental import pallas as pl
from jax.experimental.pallas import tpu as pltpu
from jax.sharding import PartitionSpec as P

HALO = 64
INNER = 2
OUTER = 2
CHUNK = 128


def dft_blocks(size):
    indices = np.arange(size)
    angles = (indices[:, None] * indices[None, :] % size).astype(np.float64) * (2.0 * math.pi / size)
    factor = np.float32(1.0 / math.sqrt(size))
    cosine = (np.cos(angles).astype(np.float32) * factor).astype(ml_dtypes.bfloat16)
    sine = (np.sin(angles).astype(np.float32) * factor).astype(ml_dtypes.bfloat16)
    forward = np.block([[cosine, sine], [-sine, cosine]])
    inverse = np.block([[cosine, -sine], [sine, cosine]])
    return forward, inverse


def dot(a, b):
    return jnp.dot(a, b, preferred_element_type=jnp.float32)


def kernel(
    stripes, tiles, patterns,
    rows_ref, amp_ref, obj_ref, probe_ref, fwd_ref, inv_ref,
    obj_out, probe_out,
    ext, grad, shifted, window, exits, misses, cols, edges, totals, probes,
    pair_in, pair_sum, tile_in, tile_sum, z_in, send_sem, recv_sem,
):
    size = probe_ref.shape[-1]
    own_rows = obj_ref.shape[1]
    s = lax.axis_index("stripe")
    t = lax.axis_index("tile")
    core = lax.rem(s, 2)
    z = s // 2
    pairs = stripes // 2
    lo, hi = HALO, HALO + own_rows
    half_w = size // 2
    used = [0]

    class Copy:
        def __init__(self, src, dst, device, sends=None, receives=None):
            n = used[0]
            used[0] += 1
            self.sends, self.receives = sends, receives
            self.make = lambda: pltpu.make_async_remote_copy(
                src_ref=src, dst_ref=dst, send_sem=send_sem.at[n], recv_sem=recv_sem.at[n],
                device_id=device, device_id_type=pl.DeviceIdType.MESH,
            )

        def start(self):
            self.guard(self.sends, lambda: self.make().start())

        def sent(self):
            self.guard(self.sends, lambda: self.make().wait_send())

        def arrived(self):
            self.guard(self.receives, lambda: self.make().wait_recv())

        def guard(self, condition, act):
            if condition is None:
                act()
            else:
                pl.when(condition)(act)

    left, right = jnp.maximum(t - 1, 0), jnp.minimum(t + 1, tiles - 1)
    above, below = jnp.maximum(s - 1, 0), jnp.minimum(s + 1, stripes - 1)
    has_left, has_right = t > 0, t < tiles - 1
    has_above, has_below = s > 0, s < stripes - 1

    def to_left(src, dst):
        return Copy(src, dst, (s, left), has_left, has_right)

    def to_right(src, dst):
        return Copy(src, dst, (s, right), has_right, has_left)

    def to_above(src, dst):
        return Copy(src, dst, (above, t), has_above, has_below)

    def to_below(src, dst):
        return Copy(src, dst, (below, t), has_below, has_above)

    def column_copies(src, step, first, last):
        return [
            to_left(
                src.at[:, lo + first : lo + last, :half_w], cols.at[step, 1, :, first:last, :]
            ),
            to_right(
                src.at[:, lo + first : lo + last, half_w:], cols.at[step, 0, :, first:last, :]
            ),
        ]

    lane = lax.broadcasted_iota(jnp.int32, (own_rows, half_w), 1)
    ext[:, :lo, :] = jnp.zeros((2, lo, size), jnp.float32)
    ext[:, hi:, :] = jnp.zeros((2, ext.shape[1] - hi, size), jnp.float32)
    for part in range(2):
        turned = pltpu.roll(obj_ref[part], HALO, 1)
        ext[part, lo:hi, :half_w] = jnp.where(lane >= HALO, turned, 0.0)
        ext[part, lo:hi, half_w:] = jnp.where(lane < HALO, turned, 0.0)
    probes[0] = probe_ref[...]

    barrier = pltpu.get_barrier_semaphore()

    def greet(device):
        pl.semaphore_signal(barrier, inc=1, device_id=device, device_id_type=pl.DeviceIdType.MESH)

    for k in range(1, tiles):
        greet((s, lax.rem(t + k, tiles)))
    for k in range(1, pairs):
        greet((lax.rem(z + k, pairs) * 2 + core, t))
    pl.when(has_above)(lambda: greet((above, t)))
    pl.when(has_below)(lambda: greet((below, t)))
    pl.semaphore_wait(
        barrier,
        tiles - 1 + pairs - 1 + has_above.astype(jnp.int32) + has_below.astype(jnp.int32),
    )

    first = column_copies(ext, 0, 0, own_rows)
    for copy in first:
        copy.start()
    pad = 4 * HALO
    shifted[:, : pad // 2, :] = jnp.zeros((2, pad // 2, size), jnp.float32)
    shifted[:, pad // 2 + size :, :] = jnp.zeros((2, pad // 2 , size), jnp.float32)
    for copy in first:
        copy.sent()
        copy.arrived()

    @pl.when(has_left)
    def _():
        ext[:, lo:hi, :half_w] += cols[0, 0]

    @pl.when(has_right)
    def _():
        ext[:, lo:hi, half_w:] += cols[0, 1]

    def row_halo():
        return [
            to_above(ext.at[:, lo : lo + HALO, :], ext.at[:, hi : hi + HALO, :]),
            to_below(ext.at[:, hi - HALO : hi, :], ext.at[:, :lo, :]),
        ]

    halo = row_halo()
    for copy in halo:
        copy.start()
    for copy in halo:
        copy.arrived()
    for copy in halo:
        copy.sent()

    offset = rows_ref[0, patterns - 1] + HALO

    def rows_from(source, start, target):
        length = target.shape[1]
        total = source.shape[1]
        for part in range(2):
            for c in range(0, size, half_w):
                block = source[part, :, c : c + half_w]
                for bit in reversed(range((2 * HALO).bit_length())):
                    turned = pltpu.roll(block, total - (1 << bit), 0)
                    block = jnp.where(((start >> bit) & 1) == 1, turned, block)
                target[part, :, c : c + half_w] = block[:length]

    def pattern_pass(index, source, top, probe, target, base, accumulate, totals_mode):
        for r in range(0, size, CHUNK):
            w_re = source[0, top + r : top + r + CHUNK, :]
            w_im = source[1, top + r : top + r + CHUNK, :]
            p_re = probe[0, r : r + CHUNK, :]
            p_im = probe[1, r : r + CHUNK, :]
            exits[r : r + CHUNK, :] = (p_re * w_re - p_im * w_im).astype(jnp.bfloat16)
            exits[size + r : size + r + CHUNK, :] = (p_re * w_im + p_im * w_re).astype(jnp.bfloat16)
        for r in range(0, size, CHUNK):
            h_re = dot(fwd_ref[r : r + CHUNK, :], exits[...]).astype(jnp.bfloat16)
            h_im = dot(fwd_ref[size + r : size + r + CHUNK, :], exits[...]).astype(jnp.bfloat16)
            spec = dot(jnp.concatenate([h_re, h_im], axis=1), inv_ref[...])
            s_re, s_im = spec[:, :size], spec[:, size:]
            power = jnp.maximum(s_re * s_re + s_im * s_im, 0.25)
            scaling = amp_ref[0, index, r : r + CHUNK, :] * lax.rsqrt(power)
            misses[r : r + CHUNK, :] = (s_re - scaling * s_re).astype(jnp.bfloat16)
            misses[size + r : size + r + CHUNK, :] = (s_im - scaling * s_im).astype(jnp.bfloat16)
        for r in range(0, size, CHUNK):
            h_re = dot(inv_ref[r : r + CHUNK, :], misses[...]).astype(jnp.bfloat16)
            h_im = dot(inv_ref[size + r : size + r + CHUNK, :], misses[...]).astype(jnp.bfloat16)
            back = dot(jnp.concatenate([h_re, h_im], axis=1), fwd_ref[...])
            b_re, b_im = back[:, :size], back[:, size:]
            p_re = probe[0, r : r + CHUNK, :]
            p_im = probe[1, r : r + CHUNK, :]
            g_re = p_re * b_re + p_im * b_im
            g_im = p_re * b_im - p_im * b_re
            where = slice(base + r, base + r + CHUNK)
            if accumulate:
                g_re = g_re + target[0, where, :]
                g_im = g_im + target[1, where, :]
            target[0, where, :] = g_re
            target[1, where, :] = g_im
            if totals_mode is not None:
                w_re = source[0, top + r : top + r + CHUNK, :]
                w_im = source[1, top + r : top + r + CHUNK, :]
                q_re = w_re * b_re + w_im * b_im
                q_im = w_re * b_im - w_im * b_re
                light = w_re * w_re + w_im * w_im
                if totals_mode:
                    q_re = q_re + totals[0, r : r + CHUNK, :]
                    q_im = q_im + totals[1, r : r + CHUNK, :]
                    light = light + totals[2, r : r + CHUNK, :]
                totals[0, r : r + CHUNK, :] = q_re
                totals[1, r : r + CHUNK, :] = q_im
                totals[2, r : r + CHUNK, :] = light

    half_rows = size // 2
    tile_rows = half_rows // tiles
    z_rows = tile_rows // pairs
    scatter_z = z_rows >= 8 and z_rows * pairs == tile_rows

    for outer in range(OUTER):
        probe = probes.at[outer]
        fresh = probes.at[outer + 1]
        p_re, p_im = probe[0], probe[1]
        step_size = 1.0 / (2.0 * patterns * jnp.max(p_re * p_re + p_im * p_im) + 1e-06)
        for inner in range(INNER):
            step = outer * INNER + inner
            last_inner = inner == INNER - 1
            final = last_inner and outer == OUTER - 1
            rows_from(ext, offset, window)
            mode = (lambda later: later) if last_inner else (lambda later: None)
            pattern_pass(patterns - 1, window, 0, probe, shifted, pad // 2, False, mode(False))
            rows_from(shifted, 2 * HALO - offset, grad)
            pattern_pass(0, ext, 0, probe, grad, 0, True, mode(True))
            up = to_above(grad.at[:, :lo, :], edges.at[step, 1])
            up.start()
            pattern_pass(1, ext, 2 * HALO, probe, grad, 2 * HALO, True, mode(True))
            down = to_below(grad.at[:, hi:, :], edges.at[step, 0])
            down.start()
            middle = column_copies(grad, step + 1, HALO, own_rows - HALO)
            for copy in middle:
                copy.start()
            if last_inner:
                pair = Copy(
                    totals.at[:, pl.ds(pl.multiple_of((1 - core) * half_rows, half_rows), half_rows), :],
                    pair_in.at[outer],
                    (s + 1 - 2 * core, t),
                )
                pair.start()
            down.arrived()

            @pl.when(has_above)
            def _():
                grad[:, lo : lo + HALO, :] += edges[step, 0]

            upper = column_copies(grad, step + 1, 0, HALO)
            for copy in upper:
                copy.start()
            up.arrived()

            @pl.when(has_below)
            def _():
                grad[:, hi - HALO : hi, :] += edges[step, 1]

            lower = column_copies(grad, step + 1, own_rows - HALO, own_rows)
            for copy in lower:
                copy.start()

            if last_inner:
                pair.arrived()
                kept = pl.ds(pl.multiple_of(core * half_rows, half_rows), half_rows)
                pair_sum[...] = totals[:, kept, :] + pair_in[outer]
                over_tiles = []
                for k in range(1, tiles):
                    to = lax.rem(t + k, tiles)
                    over_tiles.append(
                        Copy(
                            pair_sum.at[:, pl.ds(pl.multiple_of(to * tile_rows, tile_rows), tile_rows), :],
                            tile_in.at[outer, k - 1],
                            (s, to),
                        )
                    )
                    over_tiles[-1].start()

            outside_left = jnp.logical_and(jnp.logical_not(has_left), lane < HALO)
            outside_right = jnp.logical_and(jnp.logical_not(has_right), lane >= HALO)
            for part in range(2):
                ext[part, lo:hi, :half_w] -= jnp.where(
                    outside_left, 0.0, step_size * grad[part, lo:hi, :half_w]
                )
                ext[part, lo:hi, half_w:] -= jnp.where(
                    outside_right, 0.0, step_size * grad[part, lo:hi, half_w:]
                )
            for copy in middle + upper + lower:
                copy.arrived()

            @pl.when(has_left)
            def _():
                ext[:, lo:hi, :half_w] -= step_size * cols[step + 1, 0]

            @pl.when(has_right)
            def _():
                ext[:, lo:hi, half_w:] -= step_size * cols[step + 1, 1]

            if not final:
                halo = row_halo()
                for copy in halo:
                    copy.start()
            else:
                halo = []
                for part in range(2):
                    obj_out[part] = jnp.where(
                        lane < HALO,
                        pltpu.roll(ext[part, lo:hi, :half_w], HALO, 1),
                        pltpu.roll(ext[part, lo:hi, half_w:], HALO, 1),
                    )

            if last_inner:
                for copy in over_tiles:
                    copy.arrived()
                mine = pl.ds(pl.multiple_of(t * tile_rows, tile_rows), tile_rows)
                total = pair_sum[:, mine, :]
                for k in range(tiles - 1):
                    total = total + tile_in[outer, k]
                tile_sum[...] = total
                over_z = []
                for k in range(1, pairs):
                    to = lax.rem(z + k, pairs)
                    if scatter_z:
                        piece = pl.ds(pl.multiple_of(to * z_rows, z_rows), z_rows)
                        source = tile_sum.at[:, piece, :]
                    else:
                        source = tile_sum
                    over_z.append(Copy(source, z_in.at[outer, k - 1], (to * 2 + core, t)))
                    over_z[-1].start()
                for copy in over_z:
                    copy.arrived()
                start_row = core * half_rows + t * tile_rows
                if scatter_z:
                    total = tile_sum[:, pl.ds(pl.multiple_of(z * z_rows, z_rows), z_rows), :]
                    count = z_rows
                    new_row = start_row + z * z_rows
                else:
                    total = tile_sum[...]
                    count = tile_rows
                    new_row = start_row
                for k in range(pairs - 1):
                    total = total + z_in[outer, k]
                place = pl.ds(pl.multiple_of(new_row, count), count)
                fresh[:, place, :] = probe[:, place, :] - 0.5 * total[:2] / (total[2:] + 1.0)
                spread = []
                if scatter_z:
                    for k in range(1, pairs):
                        rows = fresh.at[:, place, :]
                        spread.append(Copy(rows, rows, (lax.rem(z + k, pairs) * 2 + core, t)))
                        spread[-1].start()
                    for copy in spread:
                        copy.arrived()
                rows = fresh.at[:, pl.ds(pl.multiple_of(start_row, tile_rows), tile_rows), :]
                gathers = []
                for k in range(1, tiles):
                    gathers.append(Copy(rows, rows, (s, lax.rem(t + k, tiles))))
                    gathers[-1].start()
                for copy in gathers:
                    copy.arrived()
                rows = fresh.at[:, pl.ds(pl.multiple_of(core * half_rows, half_rows), half_rows), :]
                swap = Copy(rows, rows, (s + 1 - 2 * core, t))
                swap.start()
                swap.arrived()
                for copy in [pair] + over_tiles + over_z + spread + gathers + [swap]:
                    copy.sent()

            for copy in halo:
                copy.arrived()
            for copy in halo + [up, down] + middle + upper + lower:
                copy.sent()

    probe_out[...] = probes[OUTER]


def per_device(stripes, tiles, positions, row_offsets, amplitudes, object_field, probe_field):
    patterns, size = amplitudes.shape[1], probe_field.shape[-1]
    own_rows, own_columns = object_field.shape[1:]
    forward, inverse = dft_blocks(size)
    passes = INNER * OUTER
    pairs = stripes // 2
    half_rows = size // 2
    tile_rows = half_rows // tiles
    z_rows = tile_rows // pairs
    if not (z_rows >= 8 and z_rows * pairs == tile_rows):
        z_rows = tile_rows
    count = 4 + passes * 10 + OUTER * (2 + 2 * (tiles - 1) + 2 * (pairs - 1))
    f32, bf16 = jnp.float32, jnp.bfloat16
    vmem = pl.BlockSpec(memory_space=pltpu.VMEM)
    return pl.pallas_call(
        functools.partial(kernel, stripes, tiles, patterns),
        out_shape=(
            jax.ShapeDtypeStruct(object_field.shape, f32),
            jax.ShapeDtypeStruct(probe_field.shape, f32),
        ),
        in_specs=[pl.BlockSpec(memory_space=pltpu.SMEM)] + [vmem] * 5,
        out_specs=(vmem, vmem),
        scratch_shapes=[
            pltpu.VMEM((2, own_rows + 2 * HALO , size), f32),
            pltpu.VMEM((2, own_rows + 2 * HALO, size), f32),
            pltpu.VMEM((2, size + 4 * HALO , size), f32),
            pltpu.VMEM((2, size, size), f32),
            pltpu.VMEM((2 * size, size), bf16),
            pltpu.VMEM((2 * size, size), bf16),
            pltpu.VMEM((passes + 1, 2, 2, own_rows, size // 2), f32),
            pltpu.VMEM((passes, 2, 2, HALO, size), f32),
            pltpu.VMEM((3, size, size), f32),
            pltpu.VMEM((OUTER + 1, 2, size, size), f32),
            pltpu.VMEM((OUTER, 3, half_rows, size), f32),
            pltpu.VMEM((3, half_rows, size), f32),
            pltpu.VMEM((OUTER, tiles - 1, 3, tile_rows, size), f32),
            pltpu.VMEM((3, tile_rows, size), f32),
            pltpu.VMEM((OUTER, pairs - 1, 3, z_rows, size), f32),
            pltpu.SemaphoreType.DMA((count,)),
            pltpu.SemaphoreType.DMA((count,)),
        ],
        compiler_params=pltpu.CompilerParams(
            collective_id=0, has_side_effects=True, vmem_limit_bytes=40 * 1024 * 1024
        ),
        name="refine",
    )(row_offsets, amplitudes, object_field, probe_field, jnp.asarray(forward), jnp.asarray(inverse))


def solution(mesh):
    placed = (
        P("stripe", "tile"),
        P("stripe", "tile"),
        P("stripe", "tile", None, None),
        P(None, "stripe", "tile"),
        P(),
    )
    return jax.shard_map(
        functools.partial(per_device, mesh.shape["stripe"], mesh.shape["tile"]),
        mesh=mesh,
        in_specs=placed,
        out_specs=(P(None, "stripe", "tile"), P()),
        check_vma=False,
    )
```

time: 570 us -> 142 us (0.25); the launches traced: 559 us -> 142 us
  waiting for transfers between devices: 267 us -> 0 us
  Pallas kernels: 0 us -> 134 us
  matrix products: 95.6 us -> 0 us
  starting transfers between devices: 66.3 us -> 0 us
  local copies, waits for them, and re-layouts: 70 us -> 7.35 us
  between operations: 23.2 us -> 0.65 us
  blocking collectives: 21.6 us -> 0 us
  other arithmetic: 15.4 us -> 0 us
    ppermute x32 -> x0, waiting for transfers between devices: 146 us -> none  [the longest x16 76.5 us: from_behind(): lax.ppermute(value, axis, [(source, source + steps) for source in range(f...]
    pallas_call x0 -> x1, Pallas kernels: none -> 134 us  [per_device(): pl.pallas_call(functools.partial(kernel, stripes, tiles, patterns), out_s...]
    psum x2 -> x0, waiting for transfers between devices: 108 us -> none  [per_device(): share_grad, share_light = lax.psum((share_grad, share_light), 'stripe')]
    dot_general x64 -> x0, matrix products: 95.6 us -> none  [the longest x32 56.3 us: apply_right(): jnp.einsum('pkn,nm->pkm', batch, matrix, preferred_element_type=jnp.float32)]
    ppermute x32 -> x0, starting transfers between devices: 66.1 us -> none  [the longest x16 28.6 us: from_behind(): lax.ppermute(value, axis, [(source, source + steps) for source in range(f...]
    dynamic_update_slice x12 -> x0, local copies, waits for them, and re-layouts: 34.8 us -> none  [per_device(): lax.dynamic_update_slice(gradient, before + object_grad[pattern], where)]
    all_gather x2 -> x0, blocking collectives: 21.6 us -> none  [per_device(): probe_field = lax.all_gather(new_rows, 'tile', axis=1, tiled=True)]
    reduce_scatter x4 -> x0, waiting for transfers between devices: 12.2 us -> none  [the longest x2 12.1 us: per_device(): lax.psum_scatter(grad_sum, 'tile', scatter_dimension=1, tiled=True)]
  transfers between devices with their start and end apart: 38 -> 0, of which waited for: 26 -> 0; matrix products, arithmetic and copies ran while one was open for 5% -> 0% of each run, Pallas kernels for 0% -> 0%
where the time goes in v1:
time: 142 us
  Pallas kernels  134 us (94%)
  local copies, waits for them, and re-layouts  7.35 us (5%)
    pallas_call x1, Pallas kernels, per_device(): pl.pallas_call(functools.partial(kernel, stripes, tiles, patterns), out_s...  134 us
    unnamed x14, local copies, waits for them, and re-layouts  7.35 us

profile of v1, /device:TPU:0, one launch (start us, length us, event | category | flops | bytes accessed | tf_op | source)
XLA Modules:
  0.0 141.8 jit_solution(17172216132393335884)
XLA Ops:
  0.6 0.0 copy-start
  0.6 1.1 copy-done
  1.8 0.0 copy-start.1
  1.8 1.0 copy-done.1
  2.8 0.0 copy-start.2
  2.8 1.0 copy-done.2
  3.8 0.0 copy-start.3
  3.9 1.0 copy-done.3
  4.9 0.0 copy-start.4
  4.9 0.9 copy-done.4
  5.8 0.0 copy-start.5
  5.8 0.7 copy-done.5
  6.5 133.8 %refine.1 = (f32[2,256,128]{2,1,0:T(8,128)S(1)}, f32[2,256,256]{2,1,0:T(8,128)S(1)}) custom-call(s32[1,3]{1,0:T(1,128)S(1)} %copy-done.5, f32[1,3,256,256]{3,2,1,0:T(8,128)S(1)} %copy-done, f32[2,256,128]{2,1,0:T(8,128)S(1)} %copy-done.4, f32[2,256,256]{2,1,0:T(8,128)S(1)} %copy-done.1, bf16[512,512]{1,0:T(8,128)(2,1)S(1)} %copy-done.3, ...), custom_call_target="tpu_custom_call" | custom-call | tf_op jit(solution)/shard_map/refine/pallas_call | solution.py:399
  140.3 0.7 copy.10
  141.0 0.8 copy.11
Async XLA Ops:
  0.6 1.1 copy-start
  1.8 1.0 copy-start.1
  2.8 1.0 copy-start.2
  3.8 1.0 copy-start.3
  4.9 0.9 copy-start.4
  5.8 0.7 copy-start.5

commit v2 on v1

--- a/solution.py
+++ b/solution.py
@@ -14,6 +14,7 @@
 INNER = 2
 OUTER = 2
 CHUNK = 128
+SUB = 8
 
 
 def dft_blocks(size):
@@ -33,12 +34,13 @@
 
 def kernel(
     stripes, tiles, patterns,
-    rows_ref, amp_ref, obj_ref, probe_ref, fwd_ref, inv_ref,
+    rows_ref, amp_hbm, obj_hbm, probe_hbm, fwd_hbm, inv_hbm,
     obj_out, probe_out,
+    amp_ref, obj_ref, fwd_ref, inv_ref, packed, packs,
     ext, grad, shifted, window, exits, misses, cols, edges, totals, probes,
-    pair_in, pair_sum, tile_in, tile_sum, z_in, send_sem, recv_sem,
+    pair_in, pair_sum, tile_in, tile_sum, z_in, load_sem, send_sem, recv_sem,
 ):
-    size = probe_ref.shape[-1]
+    size = probes.shape[-1]
     own_rows = obj_ref.shape[1]
     s = lax.axis_index("stripe")
     t = lax.axis_index("tile")
@@ -91,24 +93,60 @@
     def to_below(src, dst):
         return Copy(src, dst, (below, t), has_below, has_above)
 
-    def column_copies(src, step, first, last):
-        return [
-            to_left(
-                src.at[:, lo + first : lo + last, :half_w], cols.at[step, 1, :, first:last, :]
-            ),
-            to_right(
-                src.at[:, lo + first : lo + last, half_w:], cols.at[step, 0, :, first:last, :]
-            ),
+    class Columns:
+        def __init__(self, step, first, last):
+            self.step, self.first, self.last = step, first, last
+            rows = slice(lo + first, lo + last)
+            self.copies = [
+                to_left(grad.at[:, rows, :half_w], cols.at[step, 1, :, first:last, :]),
+                to_right(grad.at[:, rows, half_w:], cols.at[step, 0, :, first:last, :]),
+            ]
+            for copy in self.copies:
+                copy.start()
+
+        def receive(self, scale):
+            rows = slice(lo + self.first, lo + self.last)
+            for copy in self.copies:
+                copy.arrived()
+
+            @pl.when(has_left)
+            def _():
+                ext[:, rows, :half_w] -= scale * cols[self.step, 0, :, self.first : self.last, :]
+
+            @pl.when(has_right)
+            def _():
+                ext[:, rows, half_w:] -= scale * cols[self.step, 1, :, self.first : self.last, :]
+
+    def packed_copies(n, first, last):
+        copies = [
+            to_left(packed.at[n, 0, first:last, :], packs.at[n, 1, first:last, :]),
+            to_right(packed.at[n, 1, first:last, :], packs.at[n, 0, first:last, :]),
         ]
-
+        for copy in copies:
+            copy.start()
+        return copies
+
+    def turn(block):
+        return pltpu.roll(block, HALO, 1)
+
+    loads = [
+        pltpu.make_async_copy(source, target, load_sem.at[n])
+        for n, (source, target) in enumerate(
+            [
+                (obj_hbm, obj_ref),
+                (probe_hbm, probes.at[0]),
+                (fwd_hbm, fwd_ref),
+                (inv_hbm, inv_ref),
+                (amp_hbm, amp_ref),
+            ]
+        )
+    ]
+    for load in loads:
+        load.start()
     lane = lax.broadcasted_iota(jnp.int32, (own_rows, half_w), 1)
+    low = lane < HALO
     ext[:, :lo, :] = jnp.zeros((2, lo, size), jnp.float32)
     ext[:, hi:, :] = jnp.zeros((2, ext.shape[1] - hi, size), jnp.float32)
-    for part in range(2):
-        turned = pltpu.roll(obj_ref[part], HALO, 1)
-        ext[part, lo:hi, :half_w] = jnp.where(lane >= HALO, turned, 0.0)
-        ext[part, lo:hi, half_w:] = jnp.where(lane < HALO, turned, 0.0)
-    probes[0] = probe_ref[...]
 
     barrier = pltpu.get_barrier_semaphore()
 
@@ -126,50 +164,107 @@
         tiles - 1 + pairs - 1 + has_above.astype(jnp.int32) + has_below.astype(jnp.int32),
     )
 
-    first = column_copies(ext, 0, 0, own_rows)
-    for copy in first:
+    loads[0].wait()
+    packed[0, 0] = jnp.where(low, obj_ref[0], turn(obj_ref[1]))
+    packed[0, 1] = jnp.where(low, turn(obj_ref[0]), obj_ref[1])
+    first = [
+        packed_copies(0, 0, HALO),
+        packed_copies(0, own_rows - HALO, own_rows),
+        packed_copies(0, HALO, own_rows - HALO),
+    ]
+    for part in range(2):
+        turned = turn(obj_ref[part])
+        ext[part, lo:hi, :half_w] = jnp.where(low, 0.0, turned)
+        ext[part, lo:hi, half_w:] = jnp.where(low, turned, 0.0)
+
+    def place_columns(copies, begin, end):
+        rows = slice(lo + begin, lo + end)
+        near = low[begin:end]
+        for copy in copies:
+            copy.arrived()
+
+        @pl.when(has_left)
+        def _():
+            block = packs[0, 0, begin:end, :]
+            ext[0, rows, :half_w] = jnp.where(near, block, ext[0, rows, :half_w])
+            ext[1, rows, :half_w] = jnp.where(near, turn(block), ext[1, rows, :half_w])
+
+        @pl.when(has_right)
+        def _():
+            block = packs[0, 1, begin:end, :]
+            ext[0, rows, half_w:] = jnp.where(near, ext[0, rows, half_w:], turn(block))
+            ext[1, rows, half_w:] = jnp.where(near, ext[1, rows, half_w:], block)
+
+    def halo_above():
+        copy = to_above(ext.at[:, lo : lo + HALO, :], ext.at[:, hi : hi + HALO, :])
         copy.start()
-    pad = 4 * HALO
-    shifted[:, : pad // 2, :] = jnp.zeros((2, pad // 2, size), jnp.float32)
-    shifted[:, pad // 2 + size :, :] = jnp.zeros((2, pad // 2 , size), jnp.float32)
-    for copy in first:
-        copy.sent()
-        copy.arrived()
-
-    @pl.when(has_left)
-    def _():
-        ext[:, lo:hi, :half_w] += cols[0, 0]
-
-    @pl.when(has_right)
-    def _():
-        ext[:, lo:hi, half_w:] += cols[0, 1]
-
-    def row_halo():
-        return [
-            to_above(ext.at[:, lo : lo + HALO, :], ext.at[:, hi : hi + HALO, :]),
-            to_below(ext.at[:, hi - HALO : hi, :], ext.at[:, :lo, :]),
-        ]
-
-    halo = row_halo()
-    for copy in halo:
+        return copy
+
+    def halo_below():
+        copy = to_below(ext.at[:, hi - HALO : hi, :], ext.at[:, :lo, :])
         copy.start()
+        return copy
+
+    place_columns(first[0], 0, HALO)
+    halo = [halo_above()]
+    place_columns(first[1], own_rows - HALO, own_rows)
+    halo.append(halo_below())
+    place_columns(first[2], HALO, own_rows - HALO)
+    for load in loads[1:]:
+        load.wait()
     for copy in halo:
         copy.arrived()
-    for copy in halo:
+    for copy in halo + sum(first, []):
         copy.sent()
 
     offset = rows_ref[0, patterns - 1] + HALO
 
-    def rows_from(source, start, target):
-        length = target.shape[1]
-        total = source.shape[1]
+    top_bit = (2 * HALO).bit_length() - 1
+    whole = offset == 2 * HALO
+
+    def is_set(bit):
+        return ((offset >> bit) & 1) == 1
+
+    def rows_out():
         for part in range(2):
             for c in range(0, size, half_w):
-                block = source[part, :, c : c + half_w]
-                for bit in reversed(range((2 * HALO).bit_length())):
-                    turned = pltpu.roll(block, total - (1 << bit), 0)
-                    block = jnp.where(((start >> bit) & 1) == 1, turned, block)
-                target[part, :, c : c + half_w] = block[:length]
+                block = ext[part, :, c : c + half_w]
+                for bit in reversed(range(top_bit)):
+                    jump = 1 << bit
+                    if jump >= SUB:
+                        keep = block.shape[0] - jump
+                        block = jnp.where(is_set(bit), block[jump:], block[:keep])
+                    else:
+                        turned = pltpu.roll(block, block.shape[0] - jump, 0)
+                        block = jnp.where(is_set(bit), turned, block)
+                window[part, :, c : c + half_w] = jnp.where(
+                    whole, ext[part, 2 * HALO : 2 * HALO + size, c : c + half_w], block[:size]
+                )
+
+    def rows_in():
+        for part in range(2):
+            for c in range(0, size, half_w):
+                patch = shifted[part, :, c : c + half_w]
+
+                def zeros(rows):
+                    return jnp.zeros((rows, half_w), jnp.float32)
+
+                block = jnp.concatenate([patch, zeros(SUB)], axis=0)
+                for bit in range(top_bit):
+                    jump = 1 << bit
+                    if jump >= SUB:
+                        block = jnp.where(
+                            is_set(bit),
+                            jnp.concatenate([zeros(jump), block], axis=0),
+                            jnp.concatenate([block, zeros(jump)], axis=0),
+                        )
+                    else:
+                        block = jnp.where(is_set(bit), pltpu.roll(block, jump, 0), block)
+                grad[part, :, c : c + half_w] = jnp.where(
+                    whole,
+                    jnp.concatenate([zeros(2 * HALO), patch], axis=0),
+                    block[: size + 2 * HALO],
+                )
 
     def pattern_pass(index, source, top, probe, target, base, accumulate, totals_mode):
         for r in range(0, size, CHUNK):
@@ -231,19 +326,16 @@
             step = outer * INNER + inner
             last_inner = inner == INNER - 1
             final = last_inner and outer == OUTER - 1
-            rows_from(ext, offset, window)
+            rows_out()
             mode = (lambda later: later) if last_inner else (lambda later: None)
-            pattern_pass(patterns - 1, window, 0, probe, shifted, pad // 2, False, mode(False))
-            rows_from(shifted, 2 * HALO - offset, grad)
+            pattern_pass(patterns - 1, window, 0, probe, shifted, 0, False, mode(False))
+            rows_in()
             pattern_pass(0, ext, 0, probe, grad, 0, True, mode(True))
             up = to_above(grad.at[:, :lo, :], edges.at[step, 1])
             up.start()
             pattern_pass(1, ext, 2 * HALO, probe, grad, 2 * HALO, True, mode(True))
             down = to_below(grad.at[:, hi:, :], edges.at[step, 0])
             down.start()
-            middle = column_copies(grad, step + 1, HALO, own_rows - HALO)
-            for copy in middle:
-                copy.start()
             if last_inner:
                 pair = Copy(
                     totals.at[:, pl.ds(pl.multiple_of((1 - core) * half_rows, half_rows), half_rows), :],
@@ -251,25 +343,15 @@
                     (s + 1 - 2 * core, t),
                 )
                 pair.start()
-            down.arrived()
-
-            @pl.when(has_above)
-            def _():
-                grad[:, lo : lo + HALO, :] += edges[step, 0]
-
-            upper = column_copies(grad, step + 1, 0, HALO)
-            for copy in upper:
-                copy.start()
+            pieces = []
             up.arrived()
 
             @pl.when(has_below)
             def _():
                 grad[:, hi - HALO : hi, :] += edges[step, 1]
 
-            lower = column_copies(grad, step + 1, own_rows - HALO, own_rows)
-            for copy in lower:
-                copy.start()
-
+            if not final:
+                pieces.append(Columns(step, own_rows - HALO, own_rows))
             if last_inner:
                 pair.arrived()
                 kept = pl.ds(pl.multiple_of(core * half_rows, half_rows), half_rows)
@@ -285,9 +367,24 @@
                         )
                     )
                     over_tiles[-1].start()
-
-            outside_left = jnp.logical_and(jnp.logical_not(has_left), lane < HALO)
-            outside_right = jnp.logical_and(jnp.logical_not(has_right), lane >= HALO)
+            if not final:
+                pieces.append(Columns(step, HALO, own_rows // 2))
+            down.arrived()
+
+            @pl.when(has_above)
+            def _():
+                grad[:, lo : lo + HALO, :] += edges[step, 0]
+
+            if not final:
+                pieces.append(Columns(step, 0, HALO))
+                pieces.append(Columns(step, own_rows // 2, own_rows - HALO))
+            else:
+                packed[1, 0] = jnp.where(low, grad[0, lo:hi, :half_w], turn(grad[1, lo:hi, :half_w]))
+                packed[1, 1] = jnp.where(low, turn(grad[0, lo:hi, half_w:]), grad[1, lo:hi, half_w:])
+                last = packed_copies(1, 0, own_rows)
+
+            outside_left = jnp.logical_and(jnp.logical_not(has_left), low)
+            outside_right = jnp.logical_and(jnp.logical_not(has_right), jnp.logical_not(low))
             for part in range(2):
                 ext[part, lo:hi, :half_w] -= jnp.where(
                     outside_left, 0.0, step_size * grad[part, lo:hi, :half_w]
@@ -295,28 +392,16 @@
                 ext[part, lo:hi, half_w:] -= jnp.where(
                     outside_right, 0.0, step_size * grad[part, lo:hi, half_w:]
                 )
-            for copy in middle + upper + lower:
-                copy.arrived()
-
-            @pl.when(has_left)
-            def _():
-                ext[:, lo:hi, :half_w] -= step_size * cols[step + 1, 0]
-
-            @pl.when(has_right)
-            def _():
-                ext[:, lo:hi, half_w:] -= step_size * cols[step + 1, 1]
-
+            halo = []
             if not final:
-                halo = row_halo()
-                for copy in halo:
-                    copy.start()
+                pieces[0].receive(step_size)
+                halo.append(halo_below())
+                pieces[2].receive(step_size)
+                halo.append(halo_above())
             else:
-                halo = []
                 for part in range(2):
                     obj_out[part] = jnp.where(
-                        lane < HALO,
-                        pltpu.roll(ext[part, lo:hi, :half_w], HALO, 1),
-                        pltpu.roll(ext[part, lo:hi, half_w:], HALO, 1),
+                        low, turn(ext[part, lo:hi, :half_w]), turn(ext[part, lo:hi, half_w:])
                     )
 
             if last_inner:
@@ -337,6 +422,9 @@
                         source = tile_sum
                     over_z.append(Copy(source, z_in.at[outer, k - 1], (to * 2 + core, t)))
                     over_z[-1].start()
+                if not final:
+                    pieces[1].receive(step_size)
+                    pieces[3].receive(step_size)
                 for copy in over_z:
                     copy.arrived()
                 start_row = core * half_rows + t * tile_rows
@@ -374,9 +462,30 @@
                 for copy in [pair] + over_tiles + over_z + spread + gathers + [swap]:
                     copy.sent()
 
+            if not last_inner:
+                pieces[1].receive(step_size)
+                pieces[3].receive(step_size)
+            if final:
+                for copy in last:
+                    copy.arrived()
+
+                @pl.when(has_left)
+                def _():
+                    block = step_size * packs[1, 0]
+                    obj_out[0] -= jnp.where(low, block, 0.0)
+                    obj_out[1] -= jnp.where(low, turn(block), 0.0)
+
+                @pl.when(has_right)
+                def _():
+                    block = step_size * packs[1, 1]
+                    obj_out[0] -= jnp.where(low, 0.0, turn(block))
+                    obj_out[1] -= jnp.where(low, 0.0, block)
+
+                for copy in last:
+                    copy.sent()
             for copy in halo:
                 copy.arrived()
-            for copy in halo + [up, down] + middle + upper + lower:
+            for copy in halo + [up, down] + sum([piece.copies for piece in pieces], []):
                 copy.sent()
 
     probe_out[...] = probes[OUTER]
@@ -393,7 +502,7 @@
     z_rows = tile_rows // pairs
     if not (z_rows >= 8 and z_rows * pairs == tile_rows):
         z_rows = tile_rows
-    count = 4 + passes * 10 + OUTER * (2 + 2 * (tiles - 1) + 2 * (pairs - 1))
+    count = 8 + (passes - 1) * 12 + 4 + OUTER * (2 + 2 * (tiles - 1) + 2 * (pairs - 1))
     f32, bf16 = jnp.float32, jnp.bfloat16
     vmem = pl.BlockSpec(memory_space=pltpu.VMEM)
     return pl.pallas_call(
@@ -402,16 +511,22 @@
             jax.ShapeDtypeStruct(object_field.shape, f32),
             jax.ShapeDtypeStruct(probe_field.shape, f32),
         ),
-        in_specs=[pl.BlockSpec(memory_space=pltpu.SMEM)] + [vmem] * 5,
+        in_specs=[pl.BlockSpec(memory_space=pltpu.SMEM)] + [pl.BlockSpec(memory_space=pltpu.HBM)] * 5,
         out_specs=(vmem, vmem),
         scratch_shapes=[
-            pltpu.VMEM((2, own_rows + 2 * HALO , size), f32),
+            pltpu.VMEM(amplitudes.shape, f32),
+            pltpu.VMEM(object_field.shape, f32),
+            pltpu.VMEM(forward.shape, bf16),
+            pltpu.VMEM(inverse.shape, bf16),
+            pltpu.VMEM((2, 2, own_rows, own_columns), f32),
+            pltpu.VMEM((2, 2, own_rows, own_columns), f32),
             pltpu.VMEM((2, own_rows + 2 * HALO, size), f32),
-            pltpu.VMEM((2, size + 4 * HALO , size), f32),
+            pltpu.VMEM((2, own_rows + 2 * HALO, size), f32),
+            pltpu.VMEM((2, size, size), f32),
             pltpu.VMEM((2, size, size), f32),
             pltpu.VMEM((2 * size, size), bf16),
             pltpu.VMEM((2 * size, size), bf16),
-            pltpu.VMEM((passes + 1, 2, 2, own_rows, size // 2), f32),
+            pltpu.VMEM((passes - 1, 2, 2, own_rows, size // 2), f32),
             pltpu.VMEM((passes, 2, 2, HALO, size), f32),
             pltpu.VMEM((3, size, size), f32),
             pltpu.VMEM((OUTER + 1, 2, size, size), f32),
@@ -420,6 +535,7 @@
             pltpu.VMEM((OUTER, tiles - 1, 3, tile_rows, size), f32),
             pltpu.VMEM((3, tile_rows, size), f32),
             pltpu.VMEM((OUTER, pairs - 1, 3, z_rows, size), f32),
+            pltpu.SemaphoreType.DMA((5,)),
             pltpu.SemaphoreType.DMA((count,)),
             pltpu.SemaphoreType.DMA((count,)),
         ],

time: 142 us -> 119 us (0.84)
  Pallas kernels: 134 us -> 111 us
    pallas_call x1, Pallas kernels: 134 us -> 111 us  [per_device(): pl.pallas_call(functools.partial(kernel, stripes, tiles, patterns), out_s...]
where the time goes in v2:
time: 119 us
  Pallas kernels  111 us (93%)
  local copies, waits for them, and re-layouts  7.35 us (6%)
    pallas_call x1, Pallas kernels, per_device(): pl.pallas_call(functools.partial(kernel, stripes, tiles, patterns), out_s...  111 us
    unnamed x14, local copies, waits for them, and re-layouts  7.35 us

profile of v2, /device:TPU:0, one launch (start us, length us, event | category | flops | bytes accessed | tf_op | source)
XLA Modules:
  0.0 118.9 jit_solution(8592301113235497761)
XLA Ops:
  0.6 0.0 copy-start
  0.6 1.1 copy-done
  1.8 0.0 copy-start.1
  1.8 1.0 copy-done.1
  2.8 0.0 copy-start.2
  2.8 1.0 copy-done.2
  3.8 0.0 copy-start.3
  3.9 1.0 copy-done.3
  4.9 0.0 copy-start.4
  4.9 0.9 copy-done.4
  5.8 0.0 copy-start.5
  5.8 0.7 copy-done.5
  6.5 110.9 %refine.1 = (f32[2,256,128]{2,1,0:T(8,128)S(1)}, f32[2,256,256]{2,1,0:T(8,128)S(1)}) custom-call(s32[1,3]{1,0:T(1,128)S(1)} %copy-done.5, f32[1,3,256,256]{3,2,1,0:T(8,128)S(1)} %copy-done, f32[2,256,128]{2,1,0:T(8,128)S(1)} %copy-done.4, f32[2,256,256]{2,1,0:T(8,128)S(1)} %copy-done.1, bf16[512,512]{1,0:T(8,128)(2,1)S(1)} %copy-done.3, ...), custom_call_target="tpu_custom_call" | custom-call | tf_op jit(solution)/shard_map/refine/pallas_call | solution.py:508
  117.4 0.7 copy.10
  118.1 0.8 copy.11
Async XLA Ops:
  0.6 1.1 copy-start
  1.8 1.0 copy-start.1
  2.8 1.0 copy-start.2
  3.8 1.0 copy-start.3
  4.9 0.9 copy-start.4
  5.8 0.7 copy-start.5

commit v3 on v2

--- a/solution.py
+++ b/solution.py
@@ -13,7 +13,7 @@
 HALO = 64
 INNER = 2
 OUTER = 2
-CHUNK = 128
+CHUNK = 256
 SUB = 8
 
 
@@ -274,19 +274,19 @@
             p_im = probe[1, r : r + CHUNK, :]
             exits[r : r + CHUNK, :] = (p_re * w_re - p_im * w_im).astype(jnp.bfloat16)
             exits[size + r : size + r + CHUNK, :] = (p_re * w_im + p_im * w_re).astype(jnp.bfloat16)
+        half = dot(fwd_ref[...], exits[...]).astype(jnp.bfloat16)
+        half = jnp.concatenate([half[:size], half[size:]], axis=1)
         for r in range(0, size, CHUNK):
-            h_re = dot(fwd_ref[r : r + CHUNK, :], exits[...]).astype(jnp.bfloat16)
-            h_im = dot(fwd_ref[size + r : size + r + CHUNK, :], exits[...]).astype(jnp.bfloat16)
-            spec = dot(jnp.concatenate([h_re, h_im], axis=1), inv_ref[...])
+            spec = dot(half[r : r + CHUNK], inv_ref[...])
             s_re, s_im = spec[:, :size], spec[:, size:]
             power = jnp.maximum(s_re * s_re + s_im * s_im, 0.25)
             scaling = amp_ref[0, index, r : r + CHUNK, :] * lax.rsqrt(power)
             misses[r : r + CHUNK, :] = (s_re - scaling * s_re).astype(jnp.bfloat16)
             misses[size + r : size + r + CHUNK, :] = (s_im - scaling * s_im).astype(jnp.bfloat16)
+        half = dot(inv_ref[...], misses[...]).astype(jnp.bfloat16)
+        half = jnp.concatenate([half[:size], half[size:]], axis=1)
         for r in range(0, size, CHUNK):
-            h_re = dot(inv_ref[r : r + CHUNK, :], misses[...]).astype(jnp.bfloat16)
-            h_im = dot(inv_ref[size + r : size + r + CHUNK, :], misses[...]).astype(jnp.bfloat16)
-            back = dot(jnp.concatenate([h_re, h_im], axis=1), fwd_ref[...])
+            back = dot(half[r : r + CHUNK], fwd_ref[...])
             b_re, b_im = back[:, :size], back[:, size:]
             p_re = probe[0, r : r + CHUNK, :]
             p_im = probe[1, r : r + CHUNK, :]
@@ -540,7 +540,7 @@
             pltpu.SemaphoreType.DMA((count,)),
         ],
         compiler_params=pltpu.CompilerParams(
-            collective_id=0, has_side_effects=True, vmem_limit_bytes=40 * 1024 * 1024
+            collective_id=0, has_side_effects=True, vmem_limit_bytes=64 * 1024 * 1024
         ),
         name="refine",
     )(row_offsets, amplitudes, object_field, probe_field, jnp.asarray(forward), jnp.asarray(inverse))

time: 119 us -> 115 us (0.966)
  local copies, waits for them, and re-layouts: 7.35 us -> 2.52 us
    unnamed x14 -> x4, local copies, waits for them, and re-layouts: 7.35 us -> 2.52 us
where the time goes in v3:
time: 115 us
  Pallas kernels  111 us (97%)
  local copies, waits for them, and re-layouts  2.52 us (2%)
    pallas_call x1, Pallas kernels, per_device(): pl.pallas_call(functools.partial(kernel, stripes, tiles, patterns), out_s...  111 us
    unnamed x4, local copies, waits for them, and re-layouts  2.52 us

profile of v3, /device:TPU:0, one launch (start us, length us, event | category | flops | bytes accessed | tf_op | source)
XLA Modules:
  0.0 114.7 jit_solution(17726611152366424531)
XLA Ops:
  0.6 111.5 %refine.1 = (f32[2,256,128]{2,1,0:T(8,128)}, f32[2,256,256]{2,1,0:T(8,128)}) custom-call(s32[1,3]{1,0:T(1,128)} %rows_ref.1, f32[1,3,256,256]{3,2,1,0:T(8,128)} %amp_hbm.1, f32[2,256,128]{2,1,0:T(8,128)} %obj_hbm.1, f32[2,256,256]{2,1,0:T(8,128)} %probe_hbm.1, bf16[512,512]{1,0:T(8,128)(2,1)} %constant.4.clone.fwd_hbm, bf16[512,512]{1,0:T(8,128)(2,1)} %constant.5.clone.inv_hbm), custom_call_target="tpu_custom_call" | custom-call | tf_op jit(solution)/shard_map/refine/pallas_call | solution.py:508
  112.1 0.0 copy-start
  112.1 1.7 %copy.10 = f32[2,256,128]{2,1,0:T(8,128)} copy(f32[2,256,128]{2,1,0:T(8,128)} %get-tuple-element.4) | data formatting | bytes 524288
  113.9 0.0 copy-done
  113.9 0.8 copy.11
Async XLA Ops:
  112.1 1.7 %copy-start = (f32[2,256,256]{2,1,0:T(8,128)S(1)}, f32[2,256,256]{2,1,0:T(8,128)}, u32[]{:S(2)}) copy-start(f32[2,256,256]{2,1,0:T(8,128)} %get-tuple-element.5) | copy-start | bytes 1572868

commit v4 on v3

--- a/solution.py
+++ b/solution.py
@@ -303,19 +303,70 @@
                 w_im = source[1, top + r : top + r + CHUNK, :]
                 q_re = w_re * b_re + w_im * b_im
                 q_im = w_re * b_im - w_im * b_re
-                light = w_re * w_re + w_im * w_im
                 if totals_mode:
                     q_re = q_re + totals[0, r : r + CHUNK, :]
                     q_im = q_im + totals[1, r : r + CHUNK, :]
-                    light = light + totals[2, r : r + CHUNK, :]
                 totals[0, r : r + CHUNK, :] = q_re
                 totals[1, r : r + CHUNK, :] = q_im
-                totals[2, r : r + CHUNK, :] = light
 
     half_rows = size // 2
     tile_rows = half_rows // tiles
     z_rows = tile_rows // pairs
     scatter_z = z_rows >= 8 and z_rows * pairs == tile_rows
+
+    kept = pl.ds(pl.multiple_of(core * half_rows, half_rows), half_rows)
+    given = pl.ds(pl.multiple_of((1 - core) * half_rows, half_rows), half_rows)
+    mine = pl.ds(pl.multiple_of(t * tile_rows, tile_rows), tile_rows)
+
+    class Totals:
+        def __init__(self, outer, parts):
+            self.outer, self.parts = outer, parts
+            self.pair = Copy(
+                totals.at[parts, given, :], pair_in.at[outer, parts], (s + 1 - 2 * core, t)
+            )
+            self.pair.start()
+
+        def to_tiles(self):
+            self.pair.arrived()
+            pair_sum[self.parts] = totals[self.parts, kept, :] + pair_in[self.outer, self.parts]
+            self.over_tiles = []
+            for k in range(1, tiles):
+                to = lax.rem(t + k, tiles)
+                there = pl.ds(pl.multiple_of(to * tile_rows, tile_rows), tile_rows)
+                copy = Copy(
+                    pair_sum.at[self.parts, there, :],
+                    tile_in.at[self.outer, k - 1, self.parts],
+                    (s, to),
+                )
+                copy.start()
+                self.over_tiles.append(copy)
+
+        def to_z(self):
+            for copy in self.over_tiles:
+                copy.arrived()
+            total = pair_sum[self.parts, mine, :]
+            for k in range(tiles - 1):
+                total = total + tile_in[self.outer, k, self.parts]
+            tile_sum[self.parts] = total
+            self.over_z = []
+            for k in range(1, pairs):
+                to = lax.rem(z + k, pairs)
+                if scatter_z:
+                    there = pl.ds(pl.multiple_of(to * z_rows, z_rows), z_rows)
+                    source = tile_sum.at[self.parts, there, :]
+                else:
+                    source = tile_sum.at[self.parts]
+                copy = Copy(source, z_in.at[self.outer, k - 1, self.parts], (to * 2 + core, t))
+                copy.start()
+                self.over_z.append(copy)
+
+        def arrived(self):
+            for copy in self.over_z:
+                copy.arrived()
+
+        def sent(self):
+            for copy in [self.pair] + self.over_tiles + self.over_z:
+                copy.sent()
 
     for outer in range(OUTER):
         probe = probes.at[outer]
@@ -328,21 +379,29 @@
             final = last_inner and outer == OUTER - 1
             rows_out()
             mode = (lambda later: later) if last_inner else (lambda later: None)
+            if last_inner:
+                for r in range(0, size, CHUNK):
+                    light = 0.0
+                    for source, top in ((window, 0), (ext, 0), (ext, 2 * HALO)):
+                        w_re = source[0, top + r : top + r + CHUNK, :]
+                        w_im = source[1, top + r : top + r + CHUNK, :]
+                        light = light + (w_re * w_re + w_im * w_im)
+                    totals[2, r : r + CHUNK, :] = light
+                lights = Totals(outer, slice(2, 3))
             pattern_pass(patterns - 1, window, 0, probe, shifted, 0, False, mode(False))
             rows_in()
+            if last_inner:
+                lights.to_tiles()
             pattern_pass(0, ext, 0, probe, grad, 0, True, mode(True))
             up = to_above(grad.at[:, :lo, :], edges.at[step, 1])
             up.start()
+            if last_inner:
+                lights.to_z()
             pattern_pass(1, ext, 2 * HALO, probe, grad, 2 * HALO, True, mode(True))
             down = to_below(grad.at[:, hi:, :], edges.at[step, 0])
             down.start()
             if last_inner:
-                pair = Copy(
-                    totals.at[:, pl.ds(pl.multiple_of((1 - core) * half_rows, half_rows), half_rows), :],
-                    pair_in.at[outer],
-                    (s + 1 - 2 * core, t),
-                )
-                pair.start()
+                slopes = Totals(outer, slice(0, 2))
             pieces = []
             up.arrived()
 
@@ -353,20 +412,7 @@
             if not final:
                 pieces.append(Columns(step, own_rows - HALO, own_rows))
             if last_inner:
-                pair.arrived()
-                kept = pl.ds(pl.multiple_of(core * half_rows, half_rows), half_rows)
-                pair_sum[...] = totals[:, kept, :] + pair_in[outer]
-                over_tiles = []
-                for k in range(1, tiles):
-                    to = lax.rem(t + k, tiles)
-                    over_tiles.append(
-                        Copy(
-                            pair_sum.at[:, pl.ds(pl.multiple_of(to * tile_rows, tile_rows), tile_rows), :],
-                            tile_in.at[outer, k - 1],
-                            (s, to),
-                        )
-                    )
-                    over_tiles[-1].start()
+                slopes.to_tiles()
             if not final:
                 pieces.append(Columns(step, HALO, own_rows // 2))
             down.arrived()
@@ -405,28 +451,12 @@
                     )
 
             if last_inner:
-                for copy in over_tiles:
-                    copy.arrived()
-                mine = pl.ds(pl.multiple_of(t * tile_rows, tile_rows), tile_rows)
-                total = pair_sum[:, mine, :]
-                for k in range(tiles - 1):
-                    total = total + tile_in[outer, k]
-                tile_sum[...] = total
-                over_z = []
-                for k in range(1, pairs):
-                    to = lax.rem(z + k, pairs)
-                    if scatter_z:
-                        piece = pl.ds(pl.multiple_of(to * z_rows, z_rows), z_rows)
-                        source = tile_sum.at[:, piece, :]
-                    else:
-                        source = tile_sum
-                    over_z.append(Copy(source, z_in.at[outer, k - 1], (to * 2 + core, t)))
-                    over_z[-1].start()
+                slopes.to_z()
                 if not final:
                     pieces[1].receive(step_size)
                     pieces[3].receive(step_size)
-                for copy in over_z:
-                    copy.arrived()
+                slopes.arrived()
+                lights.arrived()
                 start_row = core * half_rows + t * tile_rows
                 if scatter_z:
                     total = tile_sum[:, pl.ds(pl.multiple_of(z * z_rows, z_rows), z_rows), :]
@@ -459,8 +489,10 @@
                 swap = Copy(rows, rows, (s + 1 - 2 * core, t))
                 swap.start()
                 swap.arrived()
-                for copy in [pair] + over_tiles + over_z + spread + gathers + [swap]:
+                for copy in spread + gathers + [swap]:
                     copy.sent()
+                slopes.sent()
+                lights.sent()
 
             if not last_inner:
                 pieces[1].receive(step_size)
@@ -502,7 +534,7 @@
     z_rows = tile_rows // pairs
     if not (z_rows >= 8 and z_rows * pairs == tile_rows):
         z_rows = tile_rows
-    count = 8 + (passes - 1) * 12 + 4 + OUTER * (2 + 2 * (tiles - 1) + 2 * (pairs - 1))
+    count = 8 + (passes - 1) * 12 + 4 + OUTER * (2 + 2 * (tiles - 1) + 2 * (pairs - 1) + tiles + pairs - 1)
     f32, bf16 = jnp.float32, jnp.bfloat16
     vmem = pl.BlockSpec(memory_space=pltpu.VMEM)
     return pl.pallas_call(

time: 115 us -> 121 us (1.052)
  Pallas kernels: 111 us -> 117 us
    pallas_call x1, Pallas kernels: 111 us -> 117 us  [per_device(): pl.pallas_call(functools.partial(kernel, stripes, tiles, patterns), out_s...]
where the time goes in v4:
time: 121 us
  Pallas kernels  117 us (97%)
  local copies, waits for them, and re-layouts  2.52 us (2%)
    pallas_call x1, Pallas kernels, per_device(): pl.pallas_call(functools.partial(kernel, stripes, tiles, patterns), out_s...  117 us
    unnamed x4, local copies, waits for them, and re-layouts  2.52 us

profile of v4, /device:TPU:0, one launch (start us, length us, event | category | flops | bytes accessed | tf_op | source)
XLA Modules:
  0.0 120.6 jit_solution(7492308720748908720)
XLA Ops:
  0.6 117.5 %refine.1 = (f32[2,256,128]{2,1,0:T(8,128)}, f32[2,256,256]{2,1,0:T(8,128)}) custom-call(s32[1,3]{1,0:T(1,128)} %rows_ref.1, f32[1,3,256,256]{3,2,1,0:T(8,128)} %amp_hbm.1, f32[2,256,128]{2,1,0:T(8,128)} %obj_hbm.1, f32[2,256,256]{2,1,0:T(8,128)} %probe_hbm.1, bf16[512,512]{1,0:T(8,128)(2,1)} %constant.4.clone.fwd_hbm, bf16[512,512]{1,0:T(8,128)(2,1)} %constant.5.clone.inv_hbm), custom_call_target="tpu_custom_call" | custom-call | tf_op jit(solution)/shard_map/refine/pallas_call | solution.py:540
  118.1 0.0 copy-start
  118.1 1.7 %copy.10 = f32[2,256,128]{2,1,0:T(8,128)} copy(f32[2,256,128]{2,1,0:T(8,128)} %get-tuple-element.4) | data formatting | bytes 524288
  119.8 0.0 copy-done
  119.8 0.8 copy.11
Async XLA Ops:
  118.1 1.7 %copy-start = (f32[2,256,256]{2,1,0:T(8,128)S(1)}, f32[2,256,256]{2,1,0:T(8,128)}, u32[]{:S(2)}) copy-start(f32[2,256,256]{2,1,0:T(8,128)} %get-tuple-element.5) | copy-start | bytes 1572868
